TPU v7x, 32 devices: a whole 2x2x4 slice. The times are simulated.
32 devices in a mesh: tm: 4 (over y, core), panel: 8 (over z, x).
Axes of the slice: x: 2, y: 2, z: 4, core: 2. Of those that a mesh axis runs over, the one named last changes fastest.
Arguments:
- pressure: float32 [4096, 16384], P('tm', 'panel'), may hold values from -6 to 6
- freq_bins: int32 [64], replicated, may hold values from 1 to 2047
- stencil_ids: int32 [4096, 16], P('panel'), may hold values from 0 to 2047
- spline_weights: float32 [4096, 16], P('panel'), may hold values from -2 to 2
- mode_forces: float32 [32, 4096], P(None, 'panel'), may hold values from -0.09375 to 0.09375
- mode_washes: float32 [32, 4096], P(None, 'panel'), may hold values from -6 to 6
Outputs:
- grams: float32 [2, 64, 32, 32], replicated
Inputs may be any that keep to these rules, and one draw needn't show every extreme that they name: `freq_bins`: frequency bins of the excitation lines, possibly repeated. `stencil_ids`: indices within the point group of the panel, group p // 512.
All inputs are finite; a program needn't handle non-finite values.
Results may differ from a plain program's by a relative error of at most 0.000073.
Values sent between devices are 32-bit elements; how exact they have to be, the bound alone decides.
A program may use at most 64 MiB of HBM per device.

v0:
```python
import math
import jax
import jax.numpy as jnp
from jax import lax
from jax.sharding import PartitionSpec as P


def dft_table(freq_bins, first, length, total):
    times = first + jnp.arange(length, dtype=jnp.int32)
    phase = freq_bins[:, None] * times[None, :] % total
    angle = 2.0 * math.pi / total * phase.astype(jnp.float32)
    scale_value = 1.0 / math.sqrt(total)
    return jnp.concatenate([jnp.cos(angle), -jnp.sin(angle)], axis=0) * scale_value


def modal_matrices(panel_spectra, forces_own, washes_own):
    weighted = panel_spectra[:, None, :] * forces_own[None, :, :]
    return lax.dot_general(
        weighted,
        washes_own,
        (((2,), (1,)), ((), ())),
        precision=lax.Precision.HIGHEST,
        preferred_element_type=jnp.float32,
    )


def spline_basis(point_ids, stencil_ids, spline_weights):

    def add_column(column, basis):
        ids_column = lax.dynamic_slice_in_dim(stencil_ids, column, 1, 1)[:, 0]
        weight_column = lax.dynamic_slice_in_dim(spline_weights, column, 1, 1)[:, 0]
        hits = point_ids[:, None] == ids_column[None, :]
        return basis + jnp.where(hits, weight_column[None, :], jnp.float32(0.0))

    start_basis = jnp.zeros((point_ids.shape[0], stencil_ids.shape[0]), jnp.float32)
    return lax.fori_loop(0, stencil_ids.shape[1], add_column, start_basis)


def body(pressure, freq_bins, stencil_ids, spline_weights, mode_forces, mode_washes):
    tm_count = lax.axis_size("tm")
    steps_local = pressure.shape[0]
    steps_total = steps_local * tm_count
    points_local = pressure.shape[1] // tm_count
    point_ids = lax.axis_index("tm") * points_local + jnp.arange(points_local, dtype=jnp.int32)
    local_table = dft_table(freq_bins, lax.axis_index("tm") * steps_local, steps_local, steps_total)
    spectra_rows = lax.psum_scatter(
        lax.dot_general(
            pressure,
            local_table,
            (((0,), (1,)), ((), ())),
            precision=lax.Precision.HIGHEST,
            preferred_element_type=jnp.float32,
        ),
        "tm",
        scatter_dimension=0,
        tiled=True,
    )
    basis = spline_basis(point_ids, stencil_ids, spline_weights)
    partial_spectra = lax.dot_general(
        spectra_rows,
        basis,
        (((0,), (0,)), ((), ())),
        precision=lax.Precision.HIGHEST,
        preferred_element_type=jnp.float32,
    )
    owned = lax.psum_scatter(partial_spectra, "tm", scatter_dimension=1, tiled=True)
    owned_width = owned.shape[1]
    begin = lax.axis_index("tm") * owned_width
    forces_own = lax.dynamic_slice_in_dim(mode_forces, begin, owned_width, 1)
    washes_own = lax.dynamic_slice_in_dim(mode_washes, begin, owned_width, 1)
    local_grams = modal_matrices(owned, forces_own, washes_own)
    summed = lax.psum(local_grams, ("tm", "panel"))
    modes = mode_forces.shape[0]
    return summed.reshape(2, -1, modes, modes)


def solution(mesh):
    placed = (
        P("tm", "panel"),
        P(),
        P("panel", None),
        P("panel", None),
        P(None, "panel"),
        P(None, "panel"),
    )
    return jax.shard_map(body, mesh=mesh, in_specs=placed, out_specs=P(), check_vma=False)
```

profile of v0, /device:TPU:0, one launch (start us, length us, event | category | flops | bytes accessed | tf_op | source)
XLA Modules:
  0.0 212.8 jit_solution(4548003467514517349)
XLA Ops:
  6.5 1.8 fusion.12
  8.3 7.8 %convolution_bitcast_fusion = f32[2048,128]{0,1:T(8,128)} fusion(f32[1024,2048]{1,0:T(8,128)} %param.8, f32[64,1024]{1,0:T(8,128)S(1)} %get-tuple-element.132, f32[64,1024]{1,0:T(8,128)S(1)} %get-tuple-element.131), kind=kOutput, calls=%fused_computation.5 | convolution fusion | flops 3221487616 | bytes 9961472 | tf_op jit(solution)/shard_map/dot_general | solution.py:47
  16.2 0.0 reduce-scatter.3.cloned.1.call-update
  16.2 0.0 reduce-scatter.5.cloned.1.call-start
  16.3 27.4 %while.14 = (s32[]{:T(128)}, f32[512,512]{1,0:T(8,128)S(1)}, s32[512,16]{0,1:T(8,128)}, f32[512,16]{0,1:T(8,128)}, s32[]{:T(128)}, /*index=5*/s32[]{:T(128)}, s32[]{:T(128)}) while((s32[]{:T(128)}, f32[512,512]{1,0:T(8,128)S(1)}, s32[512,16]{0,1:T(8,128)}, f32[512,16]{0,1:T(8,128)}, s32[]{:T(128)}, /*index=5*/s32[]{:T(128)}, ...), condition=%wide.region_2.3_spmd.clone, body=%wide.region_1.2_spmd.clone.sunk | while | flops 1049091 | bytes 2113643 | solution.py:36
  16.3 0.7 constant_dynamic-slice_fusion.5
  17.0 0.7 constant_dynamic-slice_fusion.6
  17.7 0.2 select_add_fusion.2
  18.0 0.7 constant_dynamic-slice_fusion.5
  18.7 0.7 constant_dynamic-slice_fusion.6
  19.4 0.2 select_add_fusion.2
  19.7 0.7 constant_dynamic-slice_fusion.5
  20.4 0.7 constant_dynamic-slice_fusion.6
  21.2 0.2 select_add_fusion.2
  21.4 0.7 constant_dynamic-slice_fusion.5
  22.1 0.7 constant_dynamic-slice_fusion.6
  22.9 0.2 select_add_fusion.2
  23.1 0.7 constant_dynamic-slice_fusion.5
  23.8 0.7 constant_dynamic-slice_fusion.6
  24.6 0.2 select_add_fusion.2
  24.8 0.7 constant_dynamic-slice_fusion.5
  25.6 0.7 constant_dynamic-slice_fusion.6
  26.3 0.2 select_add_fusion.2
  26.5 0.7 constant_dynamic-slice_fusion.5
  27.3 0.7 constant_dynamic-slice_fusion.6
  28.0 0.2 select_add_fusion.2
  28.3 0.7 constant_dynamic-slice_fusion.5
  29.0 0.7 constant_dynamic-slice_fusion.6
  29.7 0.2 select_add_fusion.2
  30.0 0.7 constant_dynamic-slice_fusion.5
  30.7 0.7 constant_dynamic-slice_fusion.6
  31.4 0.2 select_add_fusion.2
  31.7 0.7 constant_dynamic-slice_fusion.5
  32.4 0.7 constant_dynamic-slice_fusion.6
  33.1 0.2 select_add_fusion.2
  33.4 0.7 constant_dynamic-slice_fusion.5
  34.1 0.7 constant_dynamic-slice_fusion.6
  34.8 0.2 select_add_fusion.2
  35.1 0.7 constant_dynamic-slice_fusion.5
  35.8 0.7 constant_dynamic-slice_fusion.6
  36.6 0.2 select_add_fusion.2
  36.8 0.7 constant_dynamic-slice_fusion.5
  37.5 0.7 constant_dynamic-slice_fusion.6
  38.3 0.2 select_add_fusion.2
  38.5 0.7 constant_dynamic-slice_fusion.5
  39.2 0.7 constant_dynamic-slice_fusion.6
  40.0 0.2 select_add_fusion.2
  40.2 0.7 constant_dynamic-slice_fusion.5
  41.0 0.7 constant_dynamic-slice_fusion.6
  41.7 0.2 select_add_fusion.2
  41.9 0.7 constant_dynamic-slice_fusion.5
  42.7 0.7 constant_dynamic-slice_fusion.6
  43.4 0.2 select_add_fusion.2
  43.6 0.3 reduce-scatter.3.cloned.1.call-done
  43.9 2.4 %fusion.18 = f32[128,512]{1,0:T(8,128)} fusion(f32[512,128]{0,1:T(8,128)} %reduce-scatter.3.cloned.1.call-done, f32[512,512]{1,0:T(8,128)S(1)} %get-tuple-element.99), kind=kOutput, calls=%fused_computation.31 | convolution fusion | flops 402653184 | bytes 1572864 | tf_op jit(solution)/shard_map/dot_general | solution.py:59
  46.3 0.0 all-reduce.2.cloned.1.call-start
  46.4 0.7 constant_dynamic-slice_fusion.2
  47.1 21.8 %reduce-scatter.5.cloned.1.call-done = f32[128,128]{1,0:T(8,128)} async-done(((f32[128,512]{1,0:T(8,128)}), f32[128,128]{1,0:T(8,128)}) %reduce-scatter.5.cloned.1.call-update) | async-done | bytes 65552 | tf_op jit(solution)/shard_map/reduce_scatter | solution.py:66
  68.9 3.1 %fusion.2 = f32[128,32,32]{0,2,1:T(8,128)S(1)} fusion(f32[32,128]{1,0:T(8,128)S(1)} %constant_dynamic-slice_fusion.2, f32[128,128]{1,0:T(8,128)} %reduce-scatter.5.cloned.1.call-done, f32[32,512]{1,0:T(8,128)S(1)} %copy-done, s32[]{:T(128)S(6)} %select_n.26), kind=kOutput, calls=%fused_computation.6 | convolution fusion | flops 201850880 | bytes 622596 | tf_op jit(solution)/shard_map/dot_general | solution.py:18
  72.0 0.6 reshape.13
  72.6 1.1 copy.7
  73.8 0.0 all-reduce.2.cloned.1.call-update
  73.8 130.2 %all-reduce.2.cloned.1.call-done = f32[2,64,32,32]{1,3,2,0:T(8,128)} async-done(((f32[2,64,32,32]{1,3,2,0:T(8,128)}), f32[2,64,32,32]{1,3,2,0:T(8,128)}) %all-reduce.2.cloned.1.call-update) | async-done | bytes 524304 | tf_op jit(solution)/shard_map/psum | solution.py:72
  204.0 2.3 %copy.15 = f32[2,64,32,32]{1,3,2,0:T(8,128)} copy(f32[2,64,32,32]{1,3,2,0:T(8,128)} %all-reduce.2.cloned.1.call-done) | data formatting | bytes 1048576
  (22 shorter events, 0.1 us)
Async XLA Ops:
  6.5 62.4 %copy-start = (f32[32,512]{1,0:T(8,128)S(1)}, f32[32,512]{1,0:T(8,128)}, u32[]{:S(2)}) copy-start(f32[32,512]{1,0:T(8,128)} %param.13) | copy-start | bytes 196612
  6.5 37.4 %reduce-scatter.3.cloned.1.call-start = ((), (), s32[]{:S(2)}) async-start(), calls=%async_computation.2 | async-start | bytes 1310720 | tf_op jit(solution)/shard_map/reduce_scatter | solution.py:46
  16.2 52.7 %reduce-scatter.5.cloned.1.call-start = ((), (), s32[]{:S(2)}) async-start(), calls=%async_computation.3 | async-start | bytes 327680 | tf_op jit(solution)/shard_map/reduce_scatter | solution.py:66
  46.3 157.7 %all-reduce.2.cloned.1.call-start = ((), (), s32[]{:S(2)}) async-start(), calls=%async_computation.4 | async-start | bytes 2097152 | tf_op jit(solution)/shard_map/psum | solution.py:72
Sparse Core Ops, SparseCore 0:
  16.3 27.5 reduce-scatter.2
  46.5 22.3 reduce-scatter.4
  74.1 129.8 all-reduce.1
where the time goes:
time: 216 us; the launch traced here: 213 us
  waiting for transfers between devices  152 us (70%)
  local copies, waits for them, and re-layouts  27.9 us (13%)
  matrix products  13.3 us (6%)
  between operations  13.1 us (6%)
  other arithmetic  5.54 us (3%)
    psum x1, waiting for transfers between devices, body(): summed = lax.psum(local_grams, ('tm', 'panel'))  130 us
    reduce_scatter x1, waiting for transfers between devices, body(): lax.psum_scatter(partial_spectra, 'tm', scatter_dimension=1, tiled=True)  21.8 us
    dynamic_slice x16, local copies, waits for them, and re-layouts, add_column(): weight_column = lax.dynamic_slice_in_dim(spline_weights, column, 1, 1)[:, 0]  11.6 us
    dynamic_slice x16, local copies, waits for them, and re-layouts, add_column(): ids_column = lax.dynamic_slice_in_dim(stencil_ids, column, 1, 1)[:, 0]  11.6 us
    dot_general x1, matrix products, body(): lax.dot_general(pressure, local_table, (((0,), (1,)), ((), ())), precisio...  7.85 us
  transfers between devices with their start and end apart: 3, of which 3 were waited for; matrix products, arithmetic and copies ran while one was open for 13% of the time, Pallas kernels for 0%

commit v1 on v0

--- a/solution.py
+++ b/solution.py
@@ -69,7 +69,7 @@
     forces_own = lax.dynamic_slice_in_dim(mode_forces, begin, owned_width, 1)
     washes_own = lax.dynamic_slice_in_dim(mode_washes, begin, owned_width, 1)
     local_grams = modal_matrices(owned, forces_own, washes_own)
-    summed = lax.psum(local_grams, ("tm", "panel"))
+    summed = jnp.sum(lax.all_gather(local_grams, ("tm", "panel")), axis=0)
     modes = mode_forces.shape[0]
     return summed.reshape(2, -1, modes, modes)
 

time: 216 us -> 248 us (1.15)
  local copies, waits for them, and re-layouts: 27.9 us -> 39.7 us
  waiting for transfers between devices: 152 us -> 162 us
  other arithmetic: 5.54 us -> 14.2 us
    all_gather x0 -> x1, waiting for transfers between devices: none -> 140 us  [body(): summed = jnp.sum(lax.all_gather(local_grams, ('tm', 'panel')), axis=0)]
    psum x1 -> x0, waiting for transfers between devices: 130 us -> none  [body(): summed = lax.psum(local_grams, ('tm', 'panel'))]
    unnamed x3, local copies, waits for them, and re-layouts: 2.27 us -> 14.1 us
    reduce_sum x0 -> x1, other arithmetic: none -> 8.64 us  [body(): summed = jnp.sum(lax.all_gather(local_grams, ('tm', 'panel')), axis=0)]
  transfers between devices with their start and end apart: 3 -> 3, of which waited for: 3 -> 3; matrix products, arithmetic and copies ran while one was open for 13% -> 11% of each run, Pallas kernels for 0% -> 0%
where the time goes in v1:
time: 248 us; the launch traced here: 244 us
  waiting for transfers between devices  162 us (65%)
  local copies, waits for them, and re-layouts  39.7 us (16%)
  other arithmetic  14.2 us (6%)
  matrix products  14.1 us (6%)
  between operations  13.1 us (5%)
    all_gather x1, waiting for transfers between devices, body(): summed = jnp.sum(lax.all_gather(local_grams, ('tm', 'panel')), axis=0)  140 us
    reduce_scatter x1, waiting for transfers between devices, body(): lax.psum_scatter(partial_spectra, 'tm', scatter_dimension=1, tiled=True)  21.8 us
    unnamed x3, local copies, waits for them, and re-layouts  14.1 us
    dynamic_slice x16, local copies, waits for them, and re-layouts, add_column(): weight_column = lax.dynamic_slice_in_dim(spline_weights, column, 1, 1)[:, 0]  11.6 us
    dynamic_slice x16, local copies, waits for them, and re-layouts, add_column(): ids_column = lax.dynamic_slice_in_dim(stencil_ids, column, 1, 1)[:, 0]  11.6 us
    reduce_sum x1, other arithmetic, body(): summed = jnp.sum(lax.all_gather(local_grams, ('tm', 'panel')), axis=0)  8.64 us
    dot_general x1, matrix products, body(): lax.dot_general(pressure, local_table, (((0,), (1,)), ((), ())), precisio...  7.85 us
  transfers between devices with their start and end apart: 3, of which 3 were waited for; matrix products, arithmetic and copies ran while one was open for 11% of the time, Pallas kernels for 0%

profile of v1, /device:TPU:0, one launch (start us, length us, event | category | flops | bytes accessed | tf_op | source)
XLA Modules:
  0.0 244.1 jit_solution(11639418356745347016)
XLA Ops:
  6.5 1.8 fusion.12
  8.3 7.8 %convolution_bitcast_fusion = f32[2048,128]{0,1:T(8,128)} fusion(f32[1024,2048]{1,0:T(8,128)} %param.8, f32[64,1024]{1,0:T(8,128)S(1)} %get-tuple-element.132, f32[64,1024]{1,0:T(8,128)S(1)} %get-tuple-element.131), kind=kOutput, calls=%fused_computation.5 | convolution fusion | flops 3221487616 | bytes 9961472 | tf_op jit(solution)/shard_map/dot_general | solution.py:47
  16.2 0.0 reduce-scatter.3.cloned.1.call-update
  16.2 0.0 reduce-scatter.5.cloned.1.call-start
  16.3 27.4 %while.14 = (s32[]{:T(128)}, f32[512,512]{1,0:T(8,128)S(1)}, s32[512,16]{0,1:T(8,128)}, f32[512,16]{0,1:T(8,128)}, s32[]{:T(128)}, /*index=5*/s32[]{:T(128)}, s32[]{:T(128)}) while((s32[]{:T(128)}, f32[512,512]{1,0:T(8,128)S(1)}, s32[512,16]{0,1:T(8,128)}, f32[512,16]{0,1:T(8,128)}, s32[]{:T(128)}, /*index=5*/s32[]{:T(128)}, ...), condition=%wide.region_2.3_spmd.clone, body=%wide.region_1.2_spmd.clone.sunk | while | flops 1049091 | bytes 2113643 | solution.py:36
  16.3 0.7 constant_dynamic-slice_fusion.5
  17.0 0.7 constant_dynamic-slice_fusion.6
  17.7 0.2 select_add_fusion.2
  18.0 0.7 constant_dynamic-slice_fusion.5
  18.7 0.7 constant_dynamic-slice_fusion.6
  19.4 0.2 select_add_fusion.2
  19.7 0.7 constant_dynamic-slice_fusion.5
  20.4 0.7 constant_dynamic-slice_fusion.6
  21.2 0.2 select_add_fusion.2
  21.4 0.7 constant_dynamic-slice_fusion.5
  22.1 0.7 constant_dynamic-slice_fusion.6
  22.9 0.2 select_add_fusion.2
  23.1 0.7 constant_dynamic-slice_fusion.5
  23.8 0.7 constant_dynamic-slice_fusion.6
  24.6 0.2 select_add_fusion.2
  24.8 0.7 constant_dynamic-slice_fusion.5
  25.6 0.7 constant_dynamic-slice_fusion.6
  26.3 0.2 select_add_fusion.2
  26.5 0.7 constant_dynamic-slice_fusion.5
  27.3 0.7 constant_dynamic-slice_fusion.6
  28.0 0.2 select_add_fusion.2
  28.3 0.7 constant_dynamic-slice_fusion.5
  29.0 0.7 constant_dynamic-slice_fusion.6
  29.7 0.2 select_add_fusion.2
  30.0 0.7 constant_dynamic-slice_fusion.5
  30.7 0.7 constant_dynamic-slice_fusion.6
  31.4 0.2 select_add_fusion.2
  31.7 0.7 constant_dynamic-slice_fusion.5
  32.4 0.7 constant_dynamic-slice_fusion.6
  33.1 0.2 select_add_fusion.2
  33.4 0.7 constant_dynamic-slice_fusion.5
  34.1 0.7 constant_dynamic-slice_fusion.6
  34.8 0.2 select_add_fusion.2
  35.1 0.7 constant_dynamic-slice_fusion.5
  35.8 0.7 constant_dynamic-slice_fusion.6
  36.6 0.2 select_add_fusion.2
  36.8 0.7 constant_dynamic-slice_fusion.5
  37.5 0.7 constant_dynamic-slice_fusion.6
  38.3 0.2 select_add_fusion.2
  38.5 0.7 constant_dynamic-slice_fusion.5
  39.2 0.7 constant_dynamic-slice_fusion.6
  40.0 0.2 select_add_fusion.2
  40.2 0.7 constant_dynamic-slice_fusion.5
  41.0 0.7 constant_dynamic-slice_fusion.6
  41.7 0.2 select_add_fusion.2
  41.9 0.7 constant_dynamic-slice_fusion.5
  42.7 0.7 constant_dynamic-slice_fusion.6
  43.4 0.2 select_add_fusion.2
  43.6 0.3 reduce-scatter.3.cloned.1.call-done
  43.9 2.4 fusion.18
  46.3 0.0 all-gather.3.cloned.1.call-start
  46.4 0.7 constant_dynamic-slice_fusion.2
  47.1 21.8 %reduce-scatter.5.cloned.1.call-done = f32[128,128]{1,0:T(8,128)} async-done(((f32[128,512]{1,0:T(8,128)}), f32[128,128]{1,0:T(8,128)}) %reduce-scatter.5.cloned.1.call-update) | async-done | bytes 65552 | tf_op jit(solution)/shard_map/reduce_scatter | solution.py:66
  68.9 3.9 %fusion.2 = f32[128,32,32]{0,2,1:T(8,128)} fusion(f32[32,128]{1,0:T(8,128)S(1)} %constant_dynamic-slice_fusion.2, f32[128,128]{1,0:T(8,128)} %reduce-scatter.5.cloned.1.call-done, f32[32,512]{1,0:T(8,128)S(1)} %copy-done, s32[]{:T(128)S(6)} %select_n.26), kind=kOutput, calls=%fused_computation.6 | convolution fusion | flops 201850880 | bytes 622596 | tf_op jit(solution)/shard_map/dot_general | solution.py:18
  72.8 140.3 %all-gather.3.cloned.1.call-done = f32[4096,32,32]{0,2,1:T(8,128)} async-done(((f32[128,32,32]{0,2,1:T(8,128)}), f32[4096,32,32]{0,2,1:T(8,128)}) %all-gather.3.cloned.1.call-update) | async-done | bytes 16777232 | tf_op jit(solution)/shard_map/all_gather | solution.py:72
  213.1 14.1 %copy.8 = f32[128,8,32,128]{3,2,1,0:T(8,128)} copy(f32[128,8,32,128]{3,1,2,0:T(8,128)} %bitcast.23) | data formatting | bytes 33554432
  227.2 8.6 %reduce_sum.9 = f32[128,32,32]{0,2,1:T(8,128)S(1)} reduce(f32[32,128,32,32]{1,0,3,2:T(8,128)} %bitcast.22, f32[]{:T(128)} %constant.59.clone.1), dimensions={0}, to_apply=%region_4.5 | reduce | flops 4063232 | bytes 17301508 | tf_op jit(solution)/shard_map/reduce_sum | solution.py:72
  235.8 0.6 reshape.13
  236.5 1.1 copy.7
  (23 shorter events, 0.1 us)
Async XLA Ops:
  6.5 62.4 %copy-start = (f32[32,512]{1,0:T(8,128)S(1)}, f32[32,512]{1,0:T(8,128)}, u32[]{:S(2)}) copy-start(f32[32,512]{1,0:T(8,128)} %param.13) | copy-start | bytes 196612
  6.5 37.4 %reduce-scatter.3.cloned.1.call-start = ((), (), s32[]{:S(2)}) async-start(), calls=%async_computation.2 | async-start | bytes 1310720 | tf_op jit(solution)/shard_map/reduce_scatter | solution.py:46
  16.2 52.7 %reduce-scatter.5.cloned.1.call-start = ((), (), s32[]{:S(2)}) async-start(), calls=%async_computation.3 | async-start | bytes 327680 | tf_op jit(solution)/shard_map/reduce_scatter | solution.py:66
  46.3 166.8 %all-gather.3.cloned.1.call-start = ((), (), s32[]{:S(2)}) async-start(), calls=%async_computation.4 | async-start | bytes 17301504 | tf_op jit(solution)/shard_map/all_gather | solution.py:72
Sparse Core Ops, SparseCore 0:
  16.3 27.5 reduce-scatter.2
  46.5 22.3 reduce-scatter.4
  73.0 140.0 all-gather.2

commit v2 on v0

--- a/solution.py
+++ b/solution.py
@@ -69,7 +69,7 @@
     forces_own = lax.dynamic_slice_in_dim(mode_forces, begin, owned_width, 1)
     washes_own = lax.dynamic_slice_in_dim(mode_washes, begin, owned_width, 1)
     local_grams = modal_matrices(owned, forces_own, washes_own)
-    summed = lax.psum(local_grams, ("tm", "panel"))
+    summed = lax.psum(lax.psum(local_grams, "panel"), "tm")
     modes = mode_forces.shape[0]
     return summed.reshape(2, -1, modes, modes)
 

time: 216 us -> 196 us (0.907)
  waiting for transfers between devices: 152 us -> 130 us
    psum x1 -> x2, waiting for transfers between devices: 130 us -> 108 us  [body(): summed = lax.psum(lax.psum(local_grams, 'panel'), 'tm')]
  transfers between devices with their start and end apart: 3 -> 4, of which waited for: 3 -> 4; matrix products, arithmetic and copies ran while one was open for 13% -> 14% of each run, Pallas kernels for 0% -> 0%
where the time goes in v2:
time: 196 us; the launch traced here: 192 us
  waiting for transfers between devices  130 us (66%)
  local copies, waits for them, and re-layouts  28.9 us (15%)
  matrix products  14.1 us (7%)
  between operations  13.2 us (7%)
  other arithmetic  5.54 us (3%)
    psum x2, waiting for transfers between devices, body(): summed = lax.psum(lax.psum(local_grams, 'panel'), 'tm')  108 us
    reduce_scatter x1, waiting for transfers between devices, body(): lax.psum_scatter(partial_spectra, 'tm', scatter_dimension=1, tiled=True)  21.8 us
    dynamic_slice x16, local copies, waits for them, and re-layouts, add_column(): weight_column = lax.dynamic_slice_in_dim(spline_weights, column, 1, 1)[:, 0]  11.6 us
    dynamic_slice x16, local copies, waits for them, and re-layouts, add_column(): ids_column = lax.dynamic_slice_in_dim(stencil_ids, column, 1, 1)[:, 0]  11.6 us
    dot_general x1, matrix products, body(): lax.dot_general(pressure, local_table, (((0,), (1,)), ((), ())), precisio...  7.85 us
  transfers between devices with their start and end apart: 4, of which 4 were waited for; matrix products, arithmetic and copies ran while one was open for 14% of the time, Pallas kernels for 0%

profile of v2, /device:TPU:0, one launch (start us, length us, event | category | flops | bytes accessed | tf_op | source)
XLA Modules:
  0.0 192.5 jit_solution(14717601810612268748)
XLA Ops:
  6.5 1.8 fusion.12
  8.3 7.8 %convolution_bitcast_fusion = f32[2048,128]{0,1:T(8,128)} fusion(f32[1024,2048]{1,0:T(8,128)} %param.8, f32[64,1024]{1,0:T(8,128)S(1)} %get-tuple-element.132, f32[64,1024]{1,0:T(8,128)S(1)} %get-tuple-element.131), kind=kOutput, calls=%fused_computation.5 | convolution fusion | flops 3221487616 | bytes 9961472 | tf_op jit(solution)/shard_map/dot_general | solution.py:47
  16.2 0.0 reduce-scatter.5.cloned.1.call-start
  16.3 27.4 %while.14 = (s32[]{:T(128)}, f32[512,512]{1,0:T(8,128)S(1)}, s32[512,16]{0,1:T(8,128)}, f32[512,16]{0,1:T(8,128)}, s32[]{:T(128)}, /*index=5*/s32[]{:T(128)}, s32[]{:T(128)}) while((s32[]{:T(128)}, f32[512,512]{1,0:T(8,128)S(1)}, s32[512,16]{0,1:T(8,128)}, f32[512,16]{0,1:T(8,128)}, s32[]{:T(128)}, /*index=5*/s32[]{:T(128)}, ...), condition=%wide.region_2.3_spmd.clone, body=%wide.region_1.2_spmd.clone.sunk | while | flops 1049091 | bytes 2113643 | solution.py:36
  16.3 0.7 constant_dynamic-slice_fusion.5
  17.0 0.7 constant_dynamic-slice_fusion.6
  17.7 0.2 select_add_fusion.2
  18.0 0.7 constant_dynamic-slice_fusion.5
  18.7 0.7 constant_dynamic-slice_fusion.6
  19.4 0.2 select_add_fusion.2
  19.7 0.7 constant_dynamic-slice_fusion.5
  20.4 0.7 constant_dynamic-slice_fusion.6
  21.2 0.2 select_add_fusion.2
  21.4 0.7 constant_dynamic-slice_fusion.5
  22.1 0.7 constant_dynamic-slice_fusion.6
  22.9 0.2 select_add_fusion.2
  23.1 0.7 constant_dynamic-slice_fusion.5
  23.8 0.7 constant_dynamic-slice_fusion.6
  24.6 0.2 select_add_fusion.2
  24.8 0.7 constant_dynamic-slice_fusion.5
  25.6 0.7 constant_dynamic-slice_fusion.6
  26.3 0.2 select_add_fusion.2
  26.5 0.7 constant_dynamic-slice_fusion.5
  27.3 0.7 constant_dynamic-slice_fusion.6
  28.0 0.2 select_add_fusion.2
  28.3 0.7 constant_dynamic-slice_fusion.5
  29.0 0.7 constant_dynamic-slice_fusion.6
  29.7 0.2 select_add_fusion.2
  30.0 0.7 constant_dynamic-slice_fusion.5
  30.7 0.7 constant_dynamic-slice_fusion.6
  31.4 0.2 select_add_fusion.2
  31.7 0.7 constant_dynamic-slice_fusion.5
  32.4 0.7 constant_dynamic-slice_fusion.6
  33.1 0.2 select_add_fusion.2
  33.4 0.7 constant_dynamic-slice_fusion.5
  34.1 0.7 constant_dynamic-slice_fusion.6
  34.8 0.2 select_add_fusion.2
  35.1 0.7 constant_dynamic-slice_fusion.5
  35.8 0.7 constant_dynamic-slice_fusion.6
  36.6 0.2 select_add_fusion.2
  36.8 0.7 constant_dynamic-slice_fusion.5
  37.5 0.7 constant_dynamic-slice_fusion.6
  38.3 0.2 select_add_fusion.2
  38.5 0.7 constant_dynamic-slice_fusion.5
  39.2 0.7 constant_dynamic-slice_fusion.6
  40.0 0.2 select_add_fusion.2
  40.2 0.7 constant_dynamic-slice_fusion.5
  41.0 0.7 constant_dynamic-slice_fusion.6
  41.7 0.2 select_add_fusion.2
  41.9 0.7 constant_dynamic-slice_fusion.5
  42.7 0.7 constant_dynamic-slice_fusion.6
  43.4 0.2 select_add_fusion.2
  43.6 0.3 reduce-scatter.3.cloned.1.call-done
  43.9 2.4 %fusion.18 = f32[128,512]{1,0:T(8,128)} fusion(f32[512,128]{0,1:T(8,128)} %reduce-scatter.3.cloned.1.call-done, f32[512,512]{1,0:T(8,128)S(1)} %get-tuple-element.99), kind=kOutput, calls=%fused_computation.31 | convolution fusion | flops 402653184 | bytes 1572864 | tf_op jit(solution)/shard_map/dot_general | solution.py:59
  46.3 0.0 all-reduce.3.cloned.1.call-start
  46.4 0.7 constant_dynamic-slice_fusion.2
  47.1 21.8 %reduce-scatter.5.cloned.1.call-done = f32[128,128]{1,0:T(8,128)} async-done(((f32[128,512]{1,0:T(8,128)}), f32[128,128]{1,0:T(8,128)}) %reduce-scatter.5.cloned.1.call-update) | async-done | bytes 65552 | tf_op jit(solution)/shard_map/reduce_scatter | solution.py:66
  68.9 3.9 %fusion.2 = f32[128,32,32]{0,2,1:T(8,128)} fusion(f32[32,128]{1,0:T(8,128)S(1)} %constant_dynamic-slice_fusion.2, f32[128,128]{1,0:T(8,128)} %reduce-scatter.5.cloned.1.call-done, f32[32,512]{1,0:T(8,128)S(1)} %copy-done, s32[]{:T(128)S(6)} %select_n.26), kind=kOutput, calls=%fused_computation.6 | convolution fusion | flops 201850880 | bytes 622596 | tf_op jit(solution)/shard_map/dot_general | solution.py:18
  72.8 0.0 all-reduce.5.cloned.1.call-start
  72.9 72.5 %all-reduce.3.cloned.1.call-done = f32[128,32,32]{0,2,1:T(8,128)} async-done(((f32[128,32,32]{0,2,1:T(8,128)}), f32[128,32,32]{0,2,1:T(8,128)}) %all-reduce.3.cloned.1.call-update) | async-done | bytes 524304 | tf_op jit(solution)/shard_map/psum | solution.py:72
  145.4 1.6 reshape.13
  147.0 1.1 copy.7
  148.2 35.5 %all-reduce.5.cloned.1.call-done = f32[2,64,32,32]{1,3,2,0:T(8,128)} async-done(((f32[2,64,32,32]{1,3,2,0:T(8,128)}), f32[2,64,32,32]{1,3,2,0:T(8,128)}) %all-reduce.5.cloned.1.call-update) | async-done | bytes 524304 | tf_op jit(solution)/shard_map/psum | solution.py:72
  183.7 2.3 %copy.16 = f32[2,64,32,32]{1,3,2,0:T(8,128)} copy(f32[2,64,32,32]{1,3,2,0:T(8,128)} %all-reduce.5.cloned.1.call-done) | data formatting | bytes 1048576
  (25 shorter events, 0.1 us)
Async XLA Ops:
  6.5 62.4 %copy-start = (f32[32,512]{1,0:T(8,128)S(1)}, f32[32,512]{1,0:T(8,128)}, u32[]{:S(2)}) copy-start(f32[32,512]{1,0:T(8,128)} %param.13) | copy-start | bytes 196612
  6.5 37.4 %reduce-scatter.3.cloned.1.call-start = ((), (), s32[]{:S(2)}) async-start(), calls=%async_computation.2 | async-start | bytes 1310720 | tf_op jit(solution)/shard_map/reduce_scatter | solution.py:46
  16.2 52.7 %reduce-scatter.5.cloned.1.call-start = ((), (), s32[]{:S(2)}) async-start(), calls=%async_computation.3 | async-start | bytes 327680 | tf_op jit(solution)/shard_map/reduce_scatter | solution.py:66
  46.3 99.1 %all-reduce.3.cloned.1.call-start = ((), (), s32[]{:S(2)}) async-start(), calls=%async_computation.4 | async-start | bytes 1048576 | tf_op jit(solution)/shard_map/psum | solution.py:72
  72.8 110.8 %all-reduce.5.cloned.1.call-start = ((), (), s32[]{:S(2)}) async-start(), calls=%async_computation.5 | async-start | bytes 2097152 | tf_op jit(solution)/shard_map/psum | solution.py:72
Sparse Core Ops, SparseCore 0:
  16.3 27.5 reduce-scatter.2
  46.5 22.3 reduce-scatter.4
  73.0 72.3 all-reduce.2
  148.3 35.3 all-reduce.4
